TPU v7x, 32 devices: a whole 2x2x4 slice. The times are simulated.
32 devices in a mesh: src: 8 (over y, x, core), gz: 4 (over z).
Axes of the slice: x: 2, y: 2, z: 4, core: 2. Of those that a mesh axis runs over, the one named last changes fastest.
Arguments:
- travel_times: float32 [8, 16, 128, 256], P('src', 'gz'), may hold values from -6 to 6
- upwind_codes: int32 [8, 16, 128, 256], P('src', 'gz'), may hold values from 0 to 511
- adjoint_state: float32 [8, 16, 128, 256], P('src', 'gz'), may hold values from -6 to 6
- surface_residual: float32 [8, 128, 256], P('src'), may hold values from -6 to 6
- source_cell: int32 [8], P('src'), may hold values from 0 to 524287
- slowness: float32 [16, 128, 256], P('gz'), may hold values from 0.2 to 1
Outputs:
- adjoint_next: float32 [8, 16, 128, 256], P('src', 'gz')
- coarse_kernel: float32 [8, 64, 128], P('gz')
Inputs may be any that keep to these rules, and one draw needn't show every extreme that they name: `upwind_codes`: each code holds for x, y and z (bits 0 to 2, 3 to 5, 6 to 8) a low-side bit, a high-side bit and a double-weight bit; codes may name neighbours outside the grid.
All inputs are finite; a program needn't handle non-finite values.
Results may differ from a plain program's by a relative error of at most 0.0003.
Values sent between devices are 32-bit elements; how exact they have to be, the bound alone decides.
A program may use at most 128 MiB of HBM per device.

v0:
```python
import jax
import jax.numpy as jnp
from jax import lax
from jax.sharding import PartitionSpec as P


def extended_2(x, sides, width):
    for axis, dim in sides:
        devices, length = (lax.axis_size(axis), x.shape[dim])
        up = [(i, (i + 1) % devices) for i in range(devices - 1)]
        down = [(j, i) for i, j in up]
        last = lax.slice_in_dim(x, length - width, length, axis=dim)
        leading = lax.slice_in_dim(x, 0, width, axis=dim)
        before = lax.ppermute(last, axis, up)
        after = lax.ppermute(leading, axis, down)
        x = jnp.concatenate([before, x, after], axis=dim)
    return x


def axis_pair(centre, low_side, high_side, code_field, low_ok, high_ok):
    used_low = (code_field % 2).astype(jnp.float32)
    used_high = (code_field // 2 % 2).astype(jnp.float32)
    factor = 1.0 + (code_field // 4 % 2).astype(jnp.float32)
    weight_low = factor * used_low * low_ok * jnp.abs(centre - low_side)
    weight_high = factor * used_high * high_ok * jnp.abs(centre - high_side)
    return (weight_low, weight_high)


def local_weights(times_ext, codes_ext, centre_first, total_depth):
    centre = times_ext[:, 1:-1]
    code_layer = codes_ext[:, 1:-1]
    layer_count = centre.shape[1]
    row_count = centre.shape[2]
    col_count = centre.shape[3]
    z_position = centre_first + jnp.arange(layer_count)
    low_ok_z = (z_position >= 1).astype(jnp.float32)[None, :, None, None]
    high_ok_z = (z_position <= total_depth - 2).astype(jnp.float32)[None, :, None, None]
    y_index = jnp.arange(row_count)[None, None, :, None]
    x_index = jnp.arange(col_count)[None, None, None, :]
    padded_y = jnp.pad(centre, ((0, 0), (0, 0), (1, 1), (0, 0)))
    padded_x = jnp.pad(centre, ((0, 0), (0, 0), (0, 0), (1, 1)))
    low_z, high_z = axis_pair(
        centre, times_ext[:, :-2], times_ext[:, 2:], code_layer // 64 % 8, low_ok_z, high_ok_z
    )
    low_y, high_y = axis_pair(
        centre,
        padded_y[:, :, :-2],
        padded_y[:, :, 2:],
        code_layer // 8 % 8,
        (y_index >= 1).astype(jnp.float32),
        (y_index <= row_count - 2).astype(jnp.float32),
    )
    low_x, high_x = axis_pair(
        centre,
        padded_x[:, :, :, :-2],
        padded_x[:, :, :, 2:],
        code_layer % 8,
        (x_index >= 1).astype(jnp.float32),
        (x_index <= col_count - 2).astype(jnp.float32),
    )
    return (low_z, high_z, low_y, high_y, low_x, high_x)


def finish_sweep(middle, incoming, weights, out_first, total_depth, surface_residual, source_cell):
    low_z, high_z, low_y, high_y, low_x, high_x = weights
    incoming = incoming + jnp.pad(high_y * middle, ((0, 0), (0, 0), (1, 0), (0, 0)))[:, :, :-1]
    incoming = incoming + jnp.pad(low_y * middle, ((0, 0), (0, 0), (0, 1), (0, 0)))[:, :, 1:]
    incoming = incoming + jnp.pad(high_x * middle, ((0, 0), (0, 0), (0, 0), (1, 0)))[:, :, :, :-1]
    incoming = incoming + jnp.pad(low_x * middle, ((0, 0), (0, 0), (0, 0), (0, 1)))[:, :, :, 1:]
    diagonal = 1.0 + low_z + high_z + low_y + high_y + low_x + high_x
    layer_count = middle.shape[1]
    row_count = middle.shape[2]
    col_count = middle.shape[3]
    z_position = (out_first + jnp.arange(layer_count))[None, :, None, None]
    y_index = jnp.arange(row_count)[None, None, :, None]
    x_index = jnp.arange(col_count)[None, None, None, :]
    flat_index = (z_position * row_count + y_index) * col_count + x_index
    inside = (z_position >= 0) & (z_position < total_depth)
    keep_mask = inside & (flat_index != source_cell[:, None, None, None])
    forcing = jnp.where(z_position == 0, surface_residual[:, None, :, :], jnp.float32(0.0))
    return jnp.where(keep_mask, (forcing + incoming) / diagonal, jnp.float32(0.0))


def relax_once(adjoint, weights, out_first, total_depth, surface_residual, source_cell):
    low_z, high_z = (weights[0], weights[1])
    incoming = (high_z * adjoint)[:, :-2] + (low_z * adjoint)[:, 2:]
    inner = tuple((piece[:, 1:-1] for piece in weights))
    return finish_sweep(
        adjoint[:, 1:-1], incoming, inner, out_first, total_depth, surface_residual, source_cell
    )


def shards(travel_times, upwind_codes, adjoint_state, surface_residual, source_cell, slowness):
    depth_local = travel_times.shape[1]
    total_depth = depth_local * lax.axis_size("gz")
    slab_start = lax.axis_index("gz") * depth_local
    stacked = jnp.stack([travel_times, upwind_codes.astype(jnp.float32)])
    extended = extended_2(stacked, (("gz", 2),), 2)
    weights = local_weights(extended[0], extended[1].astype(jnp.int32), slab_start - 1, total_depth)
    adjoint = adjoint_state
    for sweep_index in range(2):
        state_ext = extended_2(adjoint, (("gz", 1),), 1)
        adjoint = relax_once(
            state_ext, weights, slab_start, total_depth, surface_residual, source_cell
        )
    product = adjoint * slowness[None]
    source_count = product.shape[0]
    row_count = product.shape[2]
    col_count = product.shape[3]
    coarse = product.reshape(
        source_count, depth_local // 2, 2, row_count // 2, 2, col_count // 2, 2
    ).mean(axis=(2, 4, 6))
    coarse_kernel = lax.psum(jnp.sum(coarse, axis=0), "src")
    return (adjoint, coarse_kernel)


def solution(mesh):
    in_specs = (
        P("src", "gz", None, None),
        P("src", "gz", None, None),
        P("src", "gz", None, None),
        P("src", None, None),
        P("src"),
        P("gz", None, None),
    )
    out_specs = (P("src", "gz", None, None), P("gz", None, None))
    return jax.shard_map(shards, mesh=mesh, in_specs=in_specs, out_specs=out_specs, check_vma=False)
```

profile of v0, /device:TPU:0, one launch (start us, length us, event | category | flops | bytes accessed | tf_op | source)
XLA Modules:
  0.0 168.9 jit_solution(1630537265260104692)
XLA Ops:
  7.2 1.7 %fusion.92 = (f32[1,1,128,256]{3,2,1,0:T(8,128)S(1)}, f32[1,1,128,256]{3,2,1,0:T(8,128)}) fusion(f32[1,4,128,256]{3,2,1,0:T(8,128)} %param.8), kind=kLoop, calls=%fused_computation.206 | loop fusion | bytes 524288 | tf_op jit(solution)/shard_map/slice | solution.py:13
  8.9 1.3 collective-permute-start.3
  10.2 5.6 %collective-permute-start.2 = (f32[1,1,128,256]{3,2,1,0:T(8,128)}, f32[1,1,128,256]{3,2,1,0:T(8,128)S(1)}, u32[]{:S(2)}, u32[]{:S(2)}) collective-permute-start(f32[1,1,128,256]{3,2,1,0:T(8,128)} %get-tuple-element.49), channel_id=1, source_target_pairs={{0,1},{1,2},{2,3},{4,5},{5,6},{6,7},{8,9},{9,10},{10,11},{12,13},{... | collective-permute-start | bytes 393224 | tf_op jit(solution)/shard_map/ppermute | solution.py:14
  15.8 1.1 convert_bitcast_fusion
  16.9 1.1 fusion.59
  18.0 3.9 %collective-permute-start = (f32[2,1,2,128,256]{4,3,2,1,0:T(8,128)S(1)}, f32[2,1,2,128,256]{4,3,2,1,0:T(8,128)S(1)}, u32[]{:S(2)}, u32[]{:S(2)}) collective-permute-start(f32[2,1,2,128,256]{4,3,2,1,0:T(8,128)S(1)} %get-tuple-element.36), channel_id=1, source_target_pairs={{0,1},{1,2},{2,3},{4,5},{5,6},{6,7},{8,9},{9,10},{10,11},{12,13},{... | collective-permute-start | bytes 1572872 | tf_op jit(solution)/shard_map/ppermute | solution.py:14
  21.9 1.3 collective-permute-start.1
  23.2 0.5 fusion.75
  23.8 0.7 add_multiply_fusion
  25.2 7.3 %collective-permute-done = f32[2,1,2,128,256]{4,3,2,1,0:T(8,128)S(1)} collective-permute-done((f32[2,1,2,128,256]{4,3,2,1,0:T(8,128)S(1)}, f32[2,1,2,128,256]{4,3,2,1,0:T(8,128)S(1)}, u32[]{:S(2)}, u32[]{:S(2)}) %collective-permute-start) | collective-permute-done | bytes 524320 | tf_op jit(solution)/shard_map/ppermute | solution.py:14
  32.5 4.1 %collective-permute-done.1 = f32[2,1,2,128,256]{4,3,2,1,0:T(8,128)S(1)} collective-permute-done((f32[2,1,2,128,256]{4,3,2,1,0:T(8,128)S(1)}, f32[2,1,2,128,256]{4,3,2,1,0:T(8,128)S(1)}, u32[]{:S(2)}, u32[]{:S(2)}) %collective-permute-start.1) | collective-permute-done | bytes 524320 | tf_op jit(solution)/shard_map/ppermute | solution.py:15
  37.1 2.0 %fusion.15 = (f32[1,6,128,256]{3,2,1,0:T(8,128)S(1)}, pred[1,6,128,256]{3,2,1,0:T(8,128)(4,1)S(1)}) fusion(f32[1,8,128,256]{3,2,1,0:T(8,128)S(1)} %get-tuple-element.32, f32[6]{0:T(128)S(1)} %get-tuple-element.53, s32[1,8,128,256]{3,2,1,0:T(8,128)S(1)} %get-tuple-element.31), kind=kLoop, calls=%fused_computation.76 | loop fusion | flops 13369344 | bytes 3342360 | tf_op jit(solution)/shard_map/mul | solution.py:24
  39.1 1.0 broadcast_compare_fusion.2
  40.1 0.8 fusion.20
  41.0 0.8 broadcast_compare_fusion.5
  41.9 0.6 broadcast_compare_fusion.1
  42.5 3.3 %fusion.11 = (f32[1,6,128,256]{3,2,1,0:T(8,128)S(1)}, f32[1,6,128,256]{3,2,1,0:T(8,128)S(1)}, f32[1,6,128,256]{3,2,1,0:T(8,128)S(1)}) fusion(f32[1,8,128,256]{3,2,1,0:T(8,128)S(1)} %get-tuple-element.32, f32[6]{0:T(128)S(1)} %get-tuple-element.54, pred[1,6,128,256]{3,2,1,0:T(8,128)(4,1)S(1)} %get-tuple-element.16, ...), kind=kLoop, calls=%fused_computation.72 | loop fusion | flops 22413312 | bytes 5111832 | tf_op jit(solution)/shard_map/mul | solution.py:25
  45.9 1.1 broadcast_compare_fusion.6
  47.1 0.5 pad_slice_fusion.4
  47.6 0.5 copy-done
  48.1 0.5 fusion.83
  49.5 0.6 fusion.78
  50.2 3.5 %collective-permute-start.4 = (f32[1,1,128,256]{3,2,1,0:T(8,128)S(1)}, f32[1,1,128,256]{3,2,1,0:T(8,128)S(1)}, u32[]{:S(2)}, u32[]{:S(2)}) collective-permute-start(f32[1,1,128,256]{3,2,1,0:T(8,128)S(1)} %get-tuple-element.43), channel_id=1, source_target_pairs={{0,1},{1,2},{2,3},{4,5},{5,6},{6,7},{8,9},{9,10},{10,11},{12,13},{... | collective-permute-start | bytes 393224 | tf_op jit(solution)/shard_map/ppermute | solution.py:14
  53.7 1.6 collective-permute-start.5
  55.5 0.7 collective-permute-done.4
  56.2 4.5 %collective-permute-done.5 = f32[1,1,128,256]{3,2,1,0:T(8,128)S(1)} collective-permute-done((f32[1,1,128,256]{3,2,1,0:T(8,128)S(1)}, f32[1,1,128,256]{3,2,1,0:T(8,128)S(1)}, u32[]{:S(2)}, u32[]{:S(2)}) %collective-permute-start.5) | collective-permute-done | bytes 131104 | tf_op jit(solution)/shard_map/ppermute | solution.py:15
  60.8 1.3 bitcast_multiply_fusion
  62.1 34.8 %reshape.154 = f32[2,2,64,2,128,2]{5,4,3,2,1,0:T(8,128)} reshape(f32[1,4,128,256]{3,2,1,0:T(8,128)S(1)} %get-tuple-element.2) | data formatting | bytes 1048576 | tf_op jit(solution)/shard_map/reshape | solution.py:110
  96.9 12.2 %reduce_sum.8 = f32[2,64,128]{2,1,0:T(8,128)S(1)} reduce(f32[2,2,64,2,128,2]{5,4,3,2,1,0:T(8,128)} %reshape.154, f32[]{:T(128)} %constant.163.clone.1), dimensions={1,3,5}, to_apply=%region_0.1 | reduce | flops 114688 | bytes 589828 | tf_op jit(solution)/shard_map/reduce_sum | solution.py:112
  109.1 0.6 broadcast_multiply_fusion
  109.8 50.8 %all-reduce.12.cloned.1.call-done = f32[2,64,128]{2,1,0:T(8,128)} async-done(((f32[2,64,128]{2,1,0:T(8,128)}), f32[2,64,128]{2,1,0:T(8,128)}) %all-reduce.12.cloned.1.call-update) | async-done | bytes 65552 | tf_op jit(solution)/shard_map/psum | solution.py:113
  160.6 1.5 copy.12
  (26 shorter events, 2.0 us)
Async XLA Ops:
  7.2 29.5 %copy-start.1 = (f32[1,4,128,256]{3,2,1,0:T(8,128)S(1)}, f32[1,4,128,256]{3,2,1,0:T(8,128)}, u32[]{:S(2)}) copy-start(f32[1,4,128,256]{3,2,1,0:T(8,128)} %param.6) | copy-start | bytes 1572868
  7.2 153.4 %all-reduce.12.cloned.1.call-start = ((), (), s32[]{:S(2)}) async-start(), calls=%async_computation | async-start | bytes 131072 | tf_op jit(solution)/shard_map/psum | solution.py:113
  8.9 40.2 %collective-permute-start.3 = (f32[1,1,128,256]{3,2,1,0:T(8,128)S(1)}, f32[1,1,128,256]{3,2,1,0:T(8,128)S(1)}, u32[]{:S(2)}, u32[]{:S(2)}) collective-permute-start(f32[1,1,128,256]{3,2,1,0:T(8,128)S(1)} %get-tuple-element.48), channel_id=1, source_target_pairs={{1,0},{2,1},{3,2},{5,4},{6,5},{7,6},{9,8},{10,9},{11,10},{13,12},{... | collective-permute-start | bytes 393224 | tf_op jit(solution)/shard_map/ppermute | solution.py:15
  10.2 15.0 %collective-permute-start.2 = (f32[1,1,128,256]{3,2,1,0:T(8,128)}, f32[1,1,128,256]{3,2,1,0:T(8,128)S(1)}, u32[]{:S(2)}, u32[]{:S(2)}) collective-permute-start(f32[1,1,128,256]{3,2,1,0:T(8,128)} %get-tuple-element.49), channel_id=1, source_target_pairs={{0,1},{1,2},{2,3},{4,5},{5,6},{6,7},{8,9},{9,10},{10,11},{12,13},{... | collective-permute-start | bytes 393224 | tf_op jit(solution)/shard_map/ppermute | solution.py:14
  18.0 14.5 %collective-permute-start = (f32[2,1,2,128,256]{4,3,2,1,0:T(8,128)S(1)}, f32[2,1,2,128,256]{4,3,2,1,0:T(8,128)S(1)}, u32[]{:S(2)}, u32[]{:S(2)}) collective-permute-start(f32[2,1,2,128,256]{4,3,2,1,0:T(8,128)S(1)} %get-tuple-element.36), channel_id=1, source_target_pairs={{0,1},{1,2},{2,3},{4,5},{5,6},{6,7},{8,9},{9,10},{10,11},{12,13},{... | collective-permute-start | bytes 1572872 | tf_op jit(solution)/shard_map/ppermute | solution.py:14
  21.9 14.7 %collective-permute-start.1 = (f32[2,1,2,128,256]{4,3,2,1,0:T(8,128)S(1)}, f32[2,1,2,128,256]{4,3,2,1,0:T(8,128)S(1)}, u32[]{:S(2)}, u32[]{:S(2)}) collective-permute-start(f32[2,1,2,128,256]{4,3,2,1,0:T(8,128)S(1)} %get-tuple-element.37), channel_id=1, source_target_pairs={{1,0},{2,1},{3,2},{5,4},{6,5},{7,6},{9,8},{10,9},{11,10},{13,12},{... | collective-permute-start | bytes 1572872 | tf_op jit(solution)/shard_map/ppermute | solution.py:15
  47.1 1.0 copy-start
  48.6 0.9 copy-start.2
  50.2 6.0 %collective-permute-start.4 = (f32[1,1,128,256]{3,2,1,0:T(8,128)S(1)}, f32[1,1,128,256]{3,2,1,0:T(8,128)S(1)}, u32[]{:S(2)}, u32[]{:S(2)}) collective-permute-start(f32[1,1,128,256]{3,2,1,0:T(8,128)S(1)} %get-tuple-element.43), channel_id=1, source_target_pairs={{0,1},{1,2},{2,3},{4,5},{5,6},{6,7},{8,9},{9,10},{10,11},{12,13},{... | collective-permute-start | bytes 393224 | tf_op jit(solution)/shard_map/ppermute | solution.py:14
  53.7 7.1 %copy-start.3 = (f32[4,128,256]{2,1,0:T(8,128)S(1)}, f32[4,128,256]{2,1,0:T(8,128)}, u32[]{:S(2)}) copy-start(f32[4,128,256]{2,1,0:T(8,128)} %param.11) | copy-start | bytes 1572868
  53.7 7.0 %collective-permute-start.5 = (f32[1,1,128,256]{3,2,1,0:T(8,128)S(1)}, f32[1,1,128,256]{3,2,1,0:T(8,128)S(1)}, u32[]{:S(2)}, u32[]{:S(2)}) collective-permute-start(f32[1,1,128,256]{3,2,1,0:T(8,128)S(1)} %get-tuple-element.44), channel_id=1, source_target_pairs={{1,0},{2,1},{3,2},{5,4},{6,5},{7,6},{9,8},{10,9},{11,10},{13,12},{... | collective-permute-start | bytes 393224 | tf_op jit(solution)/shard_map/ppermute | solution.py:15
Sparse Core Ops, SparseCore 0:
  109.9 50.6 all-reduce.11
where the time goes:
time: 169 us
  waiting for transfers between devices  67.5 us (40%)
  local copies, waits for them, and re-layouts  39.5 us (23%)
  other arithmetic  29.8 us (18%)
  starting transfers between devices  17.2 us (10%)
  between operations  15 us (9%)
    psum x1, waiting for transfers between devices, shards(): coarse_kernel = lax.psum(jnp.sum(coarse, axis=0), 'src')  50.8 us
    reshape x1, local copies, waits for them, and re-layouts, shards(): product.reshape(source_count, depth_local // 2, 2, row_count // 2, 2, col...  34.8 us
    ppermute x3, starting transfers between devices, extended_2(): before = lax.ppermute(last, axis, up)  13 us
    reduce_sum x1, other arithmetic, shards(): coarse = product.reshape(source_count, depth_local // 2, 2, row_count //...  12.2 us
    ppermute x3, waiting for transfers between devices, extended_2(): after = lax.ppermute(leading, axis, down)  8.66 us
    ppermute x3, waiting for transfers between devices, extended_2(): before = lax.ppermute(last, axis, up)  8.04 us
    ppermute x3, starting transfers between devices, extended_2(): after = lax.ppermute(leading, axis, down)  4.18 us
  transfers between devices with their start and end apart: 7, of which 5 were waited for; matrix products, arithmetic and copies ran while one was open for 9% of the time, Pallas kernels for 0%

commit v1 on v0

--- a/solution.py
+++ b/solution.py
@@ -110,7 +110,7 @@
     coarse = product.reshape(
         source_count, depth_local // 2, 2, row_count // 2, 2, col_count // 2, 2
     ).mean(axis=(2, 4, 6))
-    coarse_kernel = lax.psum(jnp.sum(coarse, axis=0), "src")
+    coarse_kernel = jnp.sum(lax.all_gather(jnp.sum(coarse, axis=0), "src"), axis=0)
     return (adjoint, coarse_kernel)
 
 

time: 169 us -> 114 us (0.67)
  waiting for transfers between devices: 67.5 us -> 16.6 us
  between operations: 15 us -> 1.57 us
  blocking collectives: 0 us -> 9.87 us
    psum x1 -> x0, waiting for transfers between devices: 50.8 us -> none  [shards(): coarse_kernel = lax.psum(jnp.sum(coarse, axis=0), 'src')]
    all_gather x0 -> x1, blocking collectives: none -> 9.87 us  [shards(): lax.all_gather(jnp.sum(coarse, axis=0), 'src')]
  transfers between devices with their start and end apart: 7 -> 6, of which waited for: 5 -> 4; matrix products, arithmetic and copies ran while one was open for 9% -> 14% of each run, Pallas kernels for 0% -> 0%
where the time goes in v1:
time: 114 us; the launch traced here: 113 us
  local copies, waits for them, and re-layouts  38 us (33%)
  other arithmetic  30.1 us (26%)
  starting transfers between devices  17.1 us (15%)
  waiting for transfers between devices  16.6 us (15%)
  blocking collectives  9.87 us (9%)
  between operations  1.57 us (1%)
    reshape x1, local copies, waits for them, and re-layouts, shards(): product.reshape(source_count, depth_local // 2, 2, row_count // 2, 2, col...  34.8 us
    ppermute x3, starting transfers between devices, extended_2(): before = lax.ppermute(last, axis, up)  13 us
    reduce_sum x1, other arithmetic, shards(): coarse = product.reshape(source_count, depth_local // 2, 2, row_count //...  12.2 us
    all_gather x1, blocking collectives, shards(): lax.all_gather(jnp.sum(coarse, axis=0), 'src')  9.87 us
    ppermute x3, waiting for transfers between devices, extended_2(): after = lax.ppermute(leading, axis, down)  8.66 us
    ppermute x3, waiting for transfers between devices, extended_2(): before = lax.ppermute(last, axis, up)  7.98 us
    ppermute x3, starting transfers between devices, extended_2(): after = lax.ppermute(leading, axis, down)  4.18 us
    mul x1, other arithmetic, axis_pair(): weight_high = factor * used_high * high_ok * jnp.abs(centre - high_side)  3.34 us
  transfers between devices with their start and end apart: 6, of which 4 were waited for; matrix products, arithmetic and copies ran while one was open for 14% of the time, Pallas kernels for 0%

profile of v1, /device:TPU:0, one launch (start us, length us, event | category | flops | bytes accessed | tf_op | source)
XLA Modules:
  0.0 113.3 jit_solution(5494402003683274815)
XLA Ops:
  0.6 1.7 %fusion.92 = (f32[1,1,128,256]{3,2,1,0:T(8,128)S(1)}, f32[1,1,128,256]{3,2,1,0:T(8,128)}) fusion(f32[1,4,128,256]{3,2,1,0:T(8,128)} %param.8), kind=kLoop, calls=%fused_computation.206 | loop fusion | bytes 524288 | tf_op jit(solution)/shard_map/slice | solution.py:13
  2.3 1.3 %collective-permute-start.3 = (f32[1,1,128,256]{3,2,1,0:T(8,128)S(1)}, f32[1,1,128,256]{3,2,1,0:T(8,128)S(1)}, u32[]{:S(2)}, u32[]{:S(2)}) collective-permute-start(f32[1,1,128,256]{3,2,1,0:T(8,128)S(1)} %get-tuple-element.48), channel_id=1, source_target_pairs={{1,0},{2,1},{3,2},{5,4},{6,5},{7,6},{9,8},{10,9},{11,10},{13,12},{... | collective-permute-start | bytes 393224 | tf_op jit(solution)/shard_map/ppermute | solution.py:15
  3.6 5.6 %collective-permute-start.2 = (f32[1,1,128,256]{3,2,1,0:T(8,128)}, f32[1,1,128,256]{3,2,1,0:T(8,128)S(1)}, u32[]{:S(2)}, u32[]{:S(2)}) collective-permute-start(f32[1,1,128,256]{3,2,1,0:T(8,128)} %get-tuple-element.49), channel_id=1, source_target_pairs={{0,1},{1,2},{2,3},{4,5},{5,6},{6,7},{8,9},{9,10},{10,11},{12,13},{... | collective-permute-start | bytes 393224 | tf_op jit(solution)/shard_map/ppermute | solution.py:14
  9.2 1.1 convert_bitcast_fusion
  10.3 1.1 fusion.59
  11.4 3.9 %collective-permute-start = (f32[2,1,2,128,256]{4,3,2,1,0:T(8,128)S(1)}, f32[2,1,2,128,256]{4,3,2,1,0:T(8,128)S(1)}, u32[]{:S(2)}, u32[]{:S(2)}) collective-permute-start(f32[2,1,2,128,256]{4,3,2,1,0:T(8,128)S(1)} %get-tuple-element.36), channel_id=1, source_target_pairs={{0,1},{1,2},{2,3},{4,5},{5,6},{6,7},{8,9},{9,10},{10,11},{12,13},{... | collective-permute-start | bytes 1572872 | tf_op jit(solution)/shard_map/ppermute | solution.py:14
  15.4 1.3 %collective-permute-start.1 = (f32[2,1,2,128,256]{4,3,2,1,0:T(8,128)S(1)}, f32[2,1,2,128,256]{4,3,2,1,0:T(8,128)S(1)}, u32[]{:S(2)}, u32[]{:S(2)}) collective-permute-start(f32[2,1,2,128,256]{4,3,2,1,0:T(8,128)S(1)} %get-tuple-element.37), channel_id=1, source_target_pairs={{1,0},{2,1},{3,2},{5,4},{6,5},{7,6},{9,8},{10,9},{11,10},{13,12},{... | collective-permute-start | bytes 1572872 | tf_op jit(solution)/shard_map/ppermute | solution.py:15
  16.7 0.5 fusion.75
  17.2 0.7 add_multiply_fusion
  18.6 7.3 %collective-permute-done = f32[2,1,2,128,256]{4,3,2,1,0:T(8,128)S(1)} collective-permute-done((f32[2,1,2,128,256]{4,3,2,1,0:T(8,128)S(1)}, f32[2,1,2,128,256]{4,3,2,1,0:T(8,128)S(1)}, u32[]{:S(2)}, u32[]{:S(2)}) %collective-permute-start) | collective-permute-done | bytes 524320 | tf_op jit(solution)/shard_map/ppermute | solution.py:14
  25.9 4.1 %collective-permute-done.1 = f32[2,1,2,128,256]{4,3,2,1,0:T(8,128)S(1)} collective-permute-done((f32[2,1,2,128,256]{4,3,2,1,0:T(8,128)S(1)}, f32[2,1,2,128,256]{4,3,2,1,0:T(8,128)S(1)}, u32[]{:S(2)}, u32[]{:S(2)}) %collective-permute-start.1) | collective-permute-done | bytes 524320 | tf_op jit(solution)/shard_map/ppermute | solution.py:15
  30.5 2.0 %fusion.15 = (f32[1,6,128,256]{3,2,1,0:T(8,128)S(1)}, pred[1,6,128,256]{3,2,1,0:T(8,128)(4,1)S(1)}) fusion(f32[1,8,128,256]{3,2,1,0:T(8,128)S(1)} %get-tuple-element.32, f32[6]{0:T(128)S(1)} %get-tuple-element.53, s32[1,8,128,256]{3,2,1,0:T(8,128)S(1)} %get-tuple-element.31), kind=kLoop, calls=%fused_computation.76 | loop fusion | flops 13369344 | bytes 3342360 | tf_op jit(solution)/shard_map/mul | solution.py:24
  32.4 1.0 broadcast_compare_fusion.2
  33.4 0.8 fusion.20
  34.4 0.8 broadcast_compare_fusion.5
  35.3 0.6 broadcast_compare_fusion.1
  35.9 3.3 %fusion.11 = (f32[1,6,128,256]{3,2,1,0:T(8,128)S(1)}, f32[1,6,128,256]{3,2,1,0:T(8,128)S(1)}, f32[1,6,128,256]{3,2,1,0:T(8,128)S(1)}) fusion(f32[1,8,128,256]{3,2,1,0:T(8,128)S(1)} %get-tuple-element.32, f32[6]{0:T(128)S(1)} %get-tuple-element.54, pred[1,6,128,256]{3,2,1,0:T(8,128)(4,1)S(1)} %get-tuple-element.16, ...), kind=kLoop, calls=%fused_computation.72 | loop fusion | flops 22413312 | bytes 5111832 | tf_op jit(solution)/shard_map/mul | solution.py:25
  39.2 1.1 broadcast_compare_fusion.6
  40.5 0.6 pad_slice_fusion.4
  41.0 0.5 copy-done
  41.5 0.6 fusion.83
  42.1 0.5 fusion.85
  43.0 0.7 fusion.78
  43.7 3.5 %collective-permute-start.4 = (f32[1,1,128,256]{3,2,1,0:T(8,128)S(1)}, f32[1,1,128,256]{3,2,1,0:T(8,128)S(1)}, u32[]{:S(2)}, u32[]{:S(2)}) collective-permute-start(f32[1,1,128,256]{3,2,1,0:T(8,128)S(1)} %get-tuple-element.43), channel_id=1, source_target_pairs={{0,1},{1,2},{2,3},{4,5},{5,6},{6,7},{8,9},{9,10},{10,11},{12,13},{... | collective-permute-start | bytes 393224 | tf_op jit(solution)/shard_map/ppermute | solution.py:14
  47.1 1.6 %collective-permute-start.5 = (f32[1,1,128,256]{3,2,1,0:T(8,128)S(1)}, f32[1,1,128,256]{3,2,1,0:T(8,128)S(1)}, u32[]{:S(2)}, u32[]{:S(2)}) collective-permute-start(f32[1,1,128,256]{3,2,1,0:T(8,128)S(1)} %get-tuple-element.44), channel_id=1, source_target_pairs={{1,0},{2,1},{3,2},{5,4},{6,5},{7,6},{9,8},{10,9},{11,10},{13,12},{... | collective-permute-start | bytes 393224 | tf_op jit(solution)/shard_map/ppermute | solution.py:15
  49.0 0.7 collective-permute-done.4
  49.6 4.5 %collective-permute-done.5 = f32[1,1,128,256]{3,2,1,0:T(8,128)S(1)} collective-permute-done((f32[1,1,128,256]{3,2,1,0:T(8,128)S(1)}, f32[1,1,128,256]{3,2,1,0:T(8,128)S(1)}, u32[]{:S(2)}, u32[]{:S(2)}) %collective-permute-start.5) | collective-permute-done | bytes 131104 | tf_op jit(solution)/shard_map/ppermute | solution.py:15
  54.2 1.4 %bitcast_multiply_fusion = (f32[1,4,128,256]{3,2,1,0:T(8,128)S(1)}, f32[1,4,128,256]{3,2,1,0:T(8,128)}) fusion(f32[4,128,256]{2,1,0:T(8,128)S(1)} %copy-done.3, f32[1,4,128,256]{3,2,1,0:T(8,128)S(1)} %get-tuple-element.6, f32[1,4,128,256]{3,2,1,0:T(8,128)S(1)} %get-tuple-element.47, f32[1,4,128,256]{3,2,1,0:T(8,128)S(1)} %get-tuple-element.46, ...), kind=kLoop, calls=%fused_computation.163 | loop fusion | flops 1966080 | bytes 6424588 | tf_op jit(solution)/shard_map/mul | solution.py:106
  55.7 34.8 %reshape.162 = f32[2,2,64,2,128,2]{5,4,3,2,1,0:T(8,128)} reshape(f32[1,4,128,256]{3,2,1,0:T(8,128)S(1)} %get-tuple-element.2) | data formatting | bytes 1048576 | tf_op jit(solution)/shard_map/reshape | solution.py:110
  90.5 12.2 %reduce_sum.16 = f32[2,64,128]{2,1,0:T(8,128)S(1)} reduce(f32[2,2,64,2,128,2]{5,4,3,2,1,0:T(8,128)} %reshape.162, f32[]{:T(128)} %constant.163.clone.1), dimensions={1,3,5}, to_apply=%region_0.1 | reduce | flops 114688 | bytes 589828 | tf_op jit(solution)/shard_map/reduce_sum | solution.py:112
  102.7 9.9 %all-gather = f32[16,64,128]{2,1,0:T(8,128)S(1)} all-gather(f32[2,64,128]{2,1,0:T(8,128)S(1)} %broadcast_multiply_fusion), channel_id=2, replica_groups=mesh['src'=8,'gz'=4] {'src'}, dimensions={0}, use_global_device_ids=true | all-gather | bytes 589824 | tf_op jit(solution)/shard_map/all_gather | solution.py:113
  112.6 0.7 reduce_sum.20
  (24 shorter events, 1.4 us)
Async XLA Ops:
  0.6 29.5 %copy-start.1 = (f32[1,4,128,256]{3,2,1,0:T(8,128)S(1)}, f32[1,4,128,256]{3,2,1,0:T(8,128)}, u32[]{:S(2)}) copy-start(f32[1,4,128,256]{3,2,1,0:T(8,128)} %param.6) | copy-start | bytes 1572868
  2.3 40.2 %collective-permute-start.3 = (f32[1,1,128,256]{3,2,1,0:T(8,128)S(1)}, f32[1,1,128,256]{3,2,1,0:T(8,128)S(1)}, u32[]{:S(2)}, u32[]{:S(2)}) collective-permute-start(f32[1,1,128,256]{3,2,1,0:T(8,128)S(1)} %get-tuple-element.48), channel_id=1, source_target_pairs={{1,0},{2,1},{3,2},{5,4},{6,5},{7,6},{9,8},{10,9},{11,10},{13,12},{... | collective-permute-start | bytes 393224 | tf_op jit(solution)/shard_map/ppermute | solution.py:15
  3.6 15.0 %collective-permute-start.2 = (f32[1,1,128,256]{3,2,1,0:T(8,128)}, f32[1,1,128,256]{3,2,1,0:T(8,128)S(1)}, u32[]{:S(2)}, u32[]{:S(2)}) collective-permute-start(f32[1,1,128,256]{3,2,1,0:T(8,128)} %get-tuple-element.49), channel_id=1, source_target_pairs={{0,1},{1,2},{2,3},{4,5},{5,6},{6,7},{8,9},{9,10},{10,11},{12,13},{... | collective-permute-start | bytes 393224 | tf_op jit(solution)/shard_map/ppermute | solution.py:14
  11.4 14.5 %collective-permute-start = (f32[2,1,2,128,256]{4,3,2,1,0:T(8,128)S(1)}, f32[2,1,2,128,256]{4,3,2,1,0:T(8,128)S(1)}, u32[]{:S(2)}, u32[]{:S(2)}) collective-permute-start(f32[2,1,2,128,256]{4,3,2,1,0:T(8,128)S(1)} %get-tuple-element.36), channel_id=1, source_target_pairs={{0,1},{1,2},{2,3},{4,5},{5,6},{6,7},{8,9},{9,10},{10,11},{12,13},{... | collective-permute-start | bytes 1572872 | tf_op jit(solution)/shard_map/ppermute | solution.py:14
  15.4 14.7 %collective-permute-start.1 = (f32[2,1,2,128,256]{4,3,2,1,0:T(8,128)S(1)}, f32[2,1,2,128,256]{4,3,2,1,0:T(8,128)S(1)}, u32[]{:S(2)}, u32[]{:S(2)}) collective-permute-start(f32[2,1,2,128,256]{4,3,2,1,0:T(8,128)S(1)} %get-tuple-element.37), channel_id=1, source_target_pairs={{1,0},{2,1},{3,2},{5,4},{6,5},{7,6},{9,8},{10,9},{11,10},{13,12},{... | collective-permute-start | bytes 1572872 | tf_op jit(solution)/shard_map/ppermute | solution.py:15
  40.4 1.0 copy-start
  42.1 0.9 copy-start.2
  43.7 6.0 %collective-permute-start.4 = (f32[1,1,128,256]{3,2,1,0:T(8,128)S(1)}, f32[1,1,128,256]{3,2,1,0:T(8,128)S(1)}, u32[]{:S(2)}, u32[]{:S(2)}) collective-permute-start(f32[1,1,128,256]{3,2,1,0:T(8,128)S(1)} %get-tuple-element.43), channel_id=1, source_target_pairs={{0,1},{1,2},{2,3},{4,5},{5,6},{6,7},{8,9},{9,10},{10,11},{12,13},{... | collective-permute-start | bytes 393224 | tf_op jit(solution)/shard_map/ppermute | solution.py:14
  47.1 7.1 %copy-start.3 = (f32[4,128,256]{2,1,0:T(8,128)S(1)}, f32[4,128,256]{2,1,0:T(8,128)}, u32[]{:S(2)}) copy-start(f32[4,128,256]{2,1,0:T(8,128)} %param.11) | copy-start | bytes 1572868
  47.1 7.0 %collective-permute-start.5 = (f32[1,1,128,256]{3,2,1,0:T(8,128)S(1)}, f32[1,1,128,256]{3,2,1,0:T(8,128)S(1)}, u32[]{:S(2)}, u32[]{:S(2)}) collective-permute-start(f32[1,1,128,256]{3,2,1,0:T(8,128)S(1)} %get-tuple-element.44), channel_id=1, source_target_pairs={{1,0},{2,1},{3,2},{5,4},{6,5},{7,6},{9,8},{10,9},{11,10},{13,12},{... | collective-permute-start | bytes 393224 | tf_op jit(solution)/shard_map/ppermute | solution.py:15
